TPU v7x, 512 devices: a whole 4x8x8 slice. The times are simulated.
512 devices in a mesh: row: 32 (over z, x), inw: 8 (over y_lo, core), outw: 2 (over y_hi).
Axes of the slice: x: 4, y: 8 (y_hi: 2, y_lo: 4; y = y_hi * 4 + y_lo), z: 8, core: 2. Of those that a mesh axis runs over, the one named last changes fastest.
Arguments:
- inputs: bfloat16 [768, 8192], P('row', ('inw', 'outw')), may hold values from -6 to 6
- out_grad: bfloat16 [768, 8192], P('row', ('inw', 'outw')), may hold values from -3 to 3
- gate_weight: bfloat16 [8192, 16384], P(('inw', 'outw'), 'row'), may hold values from -0.0625 to 0.0625
- up_weight: bfloat16 [8192, 16384], P(('inw', 'outw'), 'row'), may hold values from -0.0625 to 0.0625
- down_weight: bfloat16 [16384, 8192], P('row', ('inw', 'outw')), may hold values from -0.046875 to 0.046875
Outputs:
- grad_inputs: bfloat16 [768, 8192], P('row', ('inw', 'outw'))
- grad_gate: bfloat16 [8192, 16384], P(('inw', 'outw'), 'row')
- grad_up: bfloat16 [8192, 16384], P(('inw', 'outw'), 'row')
- grad_down: bfloat16 [16384, 8192], P('row', ('inw', 'outw'))
All inputs are finite; a program needn't handle non-finite values.
Results may differ from a plain program's by a relative error of at most 0.0049.
Values may be sent and summed in bfloat16 or wider, within the bound.
A program may use at most 64 MiB of HBM per device.

v0:
```python
import jax
import jax.numpy as jnp
from jax import lax
from jax.sharding import PartitionSpec as P


def contract_last(left, right):
    return lax.dot_general(
        left, right, (((1,), (1,)), ((), ())), preferred_element_type=jnp.float32
    )


def contract_first(left, right):
    return lax.dot_general(
        left, right, (((0,), (0,)), ((), ())), preferred_element_type=jnp.float32
    )


def swiglu_grads(gate_sum, up_sum, back_sum):
    sigmoid_gate = jax.nn.sigmoid(gate_sum)
    silu_gate = gate_sum * sigmoid_gate
    hidden = (silu_gate * up_sum).astype(jnp.bfloat16)
    gate_grad = (back_sum * up_sum * sigmoid_gate * (1.0 + gate_sum * (1.0 - sigmoid_gate))).astype(
        jnp.bfloat16
    )
    up_grad = (back_sum * silu_gate).astype(jnp.bfloat16)
    return (hidden, gate_grad, up_grad)


def per_device(inputs, out_grad, gate_weight, up_weight, down_weight):
    input_rows, grad_rows = (
        lax.all_gather(inputs, "row", axis=0, tiled=True),
        lax.all_gather(out_grad, "row", axis=0, tiled=True),
    )
    gate_part = jnp.dot(input_rows, gate_weight, preferred_element_type=jnp.float32)
    up_part = jnp.dot(input_rows, up_weight, preferred_element_type=jnp.float32)
    back_part = contract_last(grad_rows, down_weight)
    gate_sum, up_sum, back_sum = lax.psum((gate_part, up_part, back_part), ("inw", "outw"))
    hidden, gate_grad, up_grad = swiglu_grads(gate_sum, up_sum, back_sum)
    grad_down = contract_first(hidden, grad_rows).astype(jnp.bfloat16)
    grad_gate = contract_first(input_rows, gate_grad).astype(jnp.bfloat16)
    grad_up = contract_first(input_rows, up_grad).astype(jnp.bfloat16)
    grad_inputs = lax.psum_scatter(
        contract_last(gate_grad, gate_weight) + contract_last(up_grad, up_weight),
        "row",
        scatter_dimension=0,
        tiled=True,
    ).astype(jnp.bfloat16)
    return (grad_inputs, grad_gate, grad_up, grad_down)


def solution(mesh):
    in_specs = (
        P("row", ("inw", "outw")),
        P("row", ("inw", "outw")),
        P(("inw", "outw"), "row"),
        P(("inw", "outw"), "row"),
        P("row", ("inw", "outw")),
    )
    out_specs = (
        P("row", ("inw", "outw")),
        P(("inw", "outw"), "row"),
        P(("inw", "outw"), "row"),
        P("row", ("inw", "outw")),
    )
    return jax.shard_map(
        per_device, mesh=mesh, in_specs=in_specs, out_specs=out_specs, check_vma=False
    )
```

profile of v0, /device:TPU:8, one launch (start us, length us, event | category | flops | bytes accessed | tf_op | source)
XLA Modules:
  0.0 479.3 jit_solution(17125121648859528537)
XLA Ops:
  7.2 0.0 copy-start
  7.2 0.0 all-reduce.3.cloned.1.call-start
  7.2 56.1 %all_gather.7 = bf16[768,512]{1,0:T(8,128)(2,1)S(1)} all-gather(bf16[24,512]{1,0:T(8,128)(2,1)} %param.5), channel_id=1, replica_groups=mesh['row'=32,'inw'=8,'outw'=2] {'row'}, dimensions={0}, use_global_device_ids=true | all-gather | bytes 811008 | tf_op jit(solution)/shard_map/all_gather | solution.py:32
  63.3 48.7 %all_gather.6 = bf16[768,512]{1,0:T(8,128)(2,1)S(1)} all-gather(bf16[24,512]{1,0:T(8,128)(2,1)} %param.6), channel_id=1, replica_groups=mesh['row'=32,'inw'=8,'outw'=2] {'row'}, dimensions={0}, use_global_device_ids=true | all-gather | bytes 811008 | tf_op jit(solution)/shard_map/all_gather | solution.py:33
  112.0 0.0 copy-done
  112.0 0.0 copy-start.2
  112.0 1.7 fusion.7
  113.8 0.0 copy-done.2
  113.8 0.0 copy-start.3
  113.8 1.8 fusion.6
  115.6 0.0 copy-done.3
  115.6 1.7 fusion.5
  117.3 0.0 all-reduce.3.cloned.1.call-update
  117.4 0.0 reduce-scatter.2.cloned.1.call-start
  117.4 122.6 %all-reduce.3.cloned.1.call-done = (f32[768,512]{1,0:T(8,128)}, f32[768,512]{1,0:T(8,128)}, f32[768,512]{1,0:T(8,128)}) async-done(((f32[768,512]{1,0:T(8,128)}, f32[768,512]{1,0:T(8,128)}, f32[768,512]{1,0:T(8,128)}), (f32[768,512]{1,0:T(8,128)}, f32[768,512]{1,0:T(8,128)}, f32[768,512]{1,0:T(8,128)})) %all-reduce.3.cloned.1.call-update) | async-done | bytes 4718608 | tf_op jit(solution)/shard_map/psum | solution.py:38
  240.0 3.2 multiply_convert_fusion.1
  243.3 0.0 copy-start.1
  243.3 0.6 fusion.8
  243.9 0.3 copy-done.1
  244.2 1.8 convolution_add_fusion
  246.0 0.0 reduce-scatter.2.cloned.1.call-update
  246.0 0.6 fusion.1
  246.6 1.0 copy.9
  247.6 1.7 fusion.2
  249.3 1.0 copy.10
  250.3 3.3 convolution_convert_fusion
  253.7 217.4 %reduce-scatter.2.cloned.1.call-done = f32[24,512]{1,0:T(8,128)} async-done(((f32[768,512]{1,0:T(8,128)}), f32[24,512]{1,0:T(8,128)}) %reduce-scatter.2.cloned.1.call-update) | async-done | bytes 49168 | tf_op jit(solution)/shard_map/reduce_scatter | solution.py:43
  471.0 1.4 convert_element_type.29
Async XLA Ops:
  7.2 104.9 %copy-start = (bf16[512,512]{1,0:T(8,128)(2,1)S(1)}, bf16[512,512]{1,0:T(8,128)(2,1)}, u32[]{:S(2)}) copy-start(bf16[512,512]{1,0:T(8,128)(2,1)} %param.7) | copy-start | bytes 1572868
  7.2 232.9 %all-reduce.3.cloned.1.call-start = ((), (), s32[]{:S(2)}) async-start(), calls=%async_computation.2 | async-start | bytes 9437184 | tf_op jit(solution)/shard_map/psum | solution.py:38
  112.0 1.7 copy-start.2
  113.8 1.8 copy-start.3
  117.4 353.7 %reduce-scatter.2.cloned.1.call-start = ((), (), s32[]{:S(2)}) async-start(), calls=%async_computation.1 | async-start | bytes 1622016 | tf_op jit(solution)/shard_map/reduce_scatter | solution.py:43
  243.3 0.9 copy-start.1
Sparse Core Ops, SparseCore 0:
  117.5 122.5 all-reduce.2
  246.1 224.8 reduce-scatter.1
where the time goes:
time: 480 us; the launch traced here: 479 us
  waiting for transfers between devices  340 us (71%)
  blocking collectives  105 us (22%)
  between operations  14.1 us (3%)
  matrix products  13.3 us (3%)
    reduce_scatter x1, waiting for transfers between devices, per_device(): lax.psum_scatter(contract_last(gate_grad, gate_weight) + contract_last(up...  217 us
    psum x1, waiting for transfers between devices, per_device(): lax.psum((gate_part, up_part, back_part), ('inw', 'outw'))  123 us
    all_gather x1, blocking collectives, per_device(): lax.all_gather(inputs, 'row', axis=0, tiled=True)  56.1 us
    all_gather x1, blocking collectives, per_device(): lax.all_gather(out_grad, 'row', axis=0, tiled=True)  48.7 us
  transfers between devices with their start and end apart: 2, of which 2 were waited for; matrix products, arithmetic and copies ran while one was open for 2% of the time, Pallas kernels for 0%

commit v1 on v0

--- a/solution.py
+++ b/solution.py
@@ -35,7 +35,7 @@
     gate_part = jnp.dot(input_rows, gate_weight, preferred_element_type=jnp.float32)
     up_part = jnp.dot(input_rows, up_weight, preferred_element_type=jnp.float32)
     back_part = contract_last(grad_rows, down_weight)
-    gate_sum, up_sum, back_sum = lax.psum((gate_part, up_part, back_part), ("inw", "outw"))
+    gate_sum, up_sum, back_sum = lax.psum(lax.psum((gate_part, up_part, back_part), "inw"), "outw")
     hidden, gate_grad, up_grad = swiglu_grads(gate_sum, up_sum, back_sum)
     grad_down = contract_first(hidden, grad_rows).astype(jnp.bfloat16)
     grad_gate = contract_first(input_rows, gate_grad).astype(jnp.bfloat16)

time: 480 us -> 718 us (1.50)
  waiting for transfers between devices: 340 us -> 579 us
    psum x1 -> x2, waiting for transfers between devices: 123 us -> 366 us  [the longest x1 249 us: per_device(): lax.psum(lax.psum((gate_part, up_part, back_part), 'inw'), 'outw')]
  transfers between devices with their start and end apart: 2 -> 3, of which waited for: 2 -> 3; matrix products, arithmetic and copies ran while one was open for 2% -> 1% of each run, Pallas kernels for 0% -> 0%
where the time goes in v1:
time: 718 us
  waiting for transfers between devices  579 us (81%)
  blocking collectives  105 us (15%)
  between operations  13.8 us (2%)
  matrix products  13.3 us (2%)
    psum x1, waiting for transfers between devices, per_device(): lax.psum(lax.psum((gate_part, up_part, back_part), 'inw'), 'outw')  249 us
    reduce_scatter x1, waiting for transfers between devices, per_device(): lax.psum_scatter(contract_last(gate_grad, gate_weight) + contract_last(up...  213 us
    psum x1, waiting for transfers between devices, per_device(): lax.psum((gate_part, up_part, back_part), 'inw')  117 us
    all_gather x1, blocking collectives, per_device(): lax.all_gather(inputs, 'row', axis=0, tiled=True)  56.1 us
    all_gather x1, blocking collectives, per_device(): lax.all_gather(out_grad, 'row', axis=0, tiled=True)  48.7 us
  transfers between devices with their start and end apart: 3, of which 3 were waited for; matrix products, arithmetic and copies ran while one was open for 1% of the time, Pallas kernels for 0%

profile of v1, /device:TPU:8, one launch (start us, length us, event | category | flops | bytes accessed | tf_op | source)
XLA Modules:
  0.0 718.1 jit_solution(12824255875572409208)
XLA Ops:
  7.2 0.0 copy-start
  7.2 0.0 all-reduce.5.cloned.1.call-start
  7.2 56.1 %all_gather.7 = bf16[768,512]{1,0:T(8,128)(2,1)S(1)} all-gather(bf16[24,512]{1,0:T(8,128)(2,1)} %param.5), channel_id=1, replica_groups=mesh['row'=32,'inw'=8,'outw'=2] {'row'}, dimensions={0}, use_global_device_ids=true | all-gather | bytes 811008 | tf_op jit(solution)/shard_map/all_gather | solution.py:32
  63.3 48.7 %all_gather.6 = bf16[768,512]{1,0:T(8,128)(2,1)S(1)} all-gather(bf16[24,512]{1,0:T(8,128)(2,1)} %param.6), channel_id=1, replica_groups=mesh['row'=32,'inw'=8,'outw'=2] {'row'}, dimensions={0}, use_global_device_ids=true | all-gather | bytes 811008 | tf_op jit(solution)/shard_map/all_gather | solution.py:33
  112.0 0.0 copy-done
  112.0 0.0 copy-start.2
  112.0 1.7 fusion.7
  113.8 0.0 copy-done.2
  113.8 0.0 copy-start.3
  113.8 1.8 fusion.6
  115.6 0.0 copy-done.3
  115.6 1.8 fusion.5
  117.3 0.0 all-reduce.5.cloned.1.call-update
  117.3 0.0 all-reduce.7.cloned.1.call-start
  117.4 117.4 %all-reduce.5.cloned.1.call-done = (f32[768,512]{1,0:T(8,128)}, f32[768,512]{1,0:T(8,128)}, f32[768,512]{1,0:T(8,128)}) async-done(((f32[768,512]{1,0:T(8,128)}, f32[768,512]{1,0:T(8,128)}, f32[768,512]{1,0:T(8,128)}), (f32[768,512]{1,0:T(8,128)}, f32[768,512]{1,0:T(8,128)}, f32[768,512]{1,0:T(8,128)})) %all-reduce.5.cloned.1.call-update) | async-done | bytes 4718608 | tf_op jit(solution)/shard_map/psum | solution.py:38
  234.7 0.0 all-reduce.7.cloned.1.call-update
  234.8 0.0 reduce-scatter.2.cloned.1.call-start
  234.8 248.9 %all-reduce.7.cloned.1.call-done = (f32[768,512]{1,0:T(8,128)}, f32[768,512]{1,0:T(8,128)}, f32[768,512]{1,0:T(8,128)}) async-done(((f32[768,512]{1,0:T(8,128)}, f32[768,512]{1,0:T(8,128)}, f32[768,512]{1,0:T(8,128)}), (f32[768,512]{1,0:T(8,128)}, f32[768,512]{1,0:T(8,128)}, f32[768,512]{1,0:T(8,128)})) %all-reduce.7.cloned.1.call-update) | async-done | bytes 4718608 | tf_op jit(solution)/shard_map/psum | solution.py:38
  483.7 3.2 multiply_convert_fusion.1
  486.9 0.0 copy-start.1
  486.9 0.6 fusion.8
  487.5 0.3 copy-done.1
  487.8 1.8 convolution_add_fusion
  489.6 0.0 reduce-scatter.2.cloned.1.call-update
  489.6 0.6 fusion.1
  490.2 1.0 copy.9
  491.3 1.7 fusion.2
  493.0 1.0 copy.10
  494.0 3.3 convolution_convert_fusion
  497.3 212.9 %reduce-scatter.2.cloned.1.call-done = f32[24,512]{1,0:T(8,128)} async-done(((f32[768,512]{1,0:T(8,128)}), f32[24,512]{1,0:T(8,128)}) %reduce-scatter.2.cloned.1.call-update) | async-done | bytes 49168 | tf_op jit(solution)/shard_map/reduce_scatter | solution.py:43
  710.2 1.4 convert_element_type.29
Async XLA Ops:
  7.2 104.9 %copy-start = (bf16[512,512]{1,0:T(8,128)(2,1)S(1)}, bf16[512,512]{1,0:T(8,128)(2,1)}, u32[]{:S(2)}) copy-start(bf16[512,512]{1,0:T(8,128)(2,1)} %param.7) | copy-start | bytes 1572868
  7.2 227.6 %all-reduce.5.cloned.1.call-start = ((), (), s32[]{:S(2)}) async-start(), calls=%async_computation.2 | async-start | bytes 9437184 | tf_op jit(solution)/shard_map/psum | solution.py:38
  112.0 1.7 copy-start.2
  113.8 1.8 copy-start.3
  117.3 366.3 %all-reduce.7.cloned.1.call-start = ((), (), s32[]{:S(2)}) async-start(), calls=%async_computation.3 | async-start | bytes 9437184 | tf_op jit(solution)/shard_map/psum | solution.py:38
  234.8 475.4 %reduce-scatter.2.cloned.1.call-start = ((), (), s32[]{:S(2)}) async-start(), calls=%async_computation.1 | async-start | bytes 1622016 | tf_op jit(solution)/shard_map/reduce_scatter | solution.py:43
  486.9 0.9 copy-start.1
Sparse Core Ops, SparseCore 0:
  117.5 117.2 all-reduce.4
  238.0 245.5 all-reduce.6
  489.8 220.3 reduce-scatter.1

commit v2 on v0

--- a/solution.py
+++ b/solution.py
@@ -2,6 +2,14 @@
 import jax.numpy as jnp
 from jax import lax
 from jax.sharding import PartitionSpec as P
+
+
+def gather_from_all(array, axis, dim):
+    devices = lax.axis_size(axis)
+    repeats = [devices if d == dim else 1 for d in range(array.ndim)]
+    return lax.all_to_all(
+        jnp.tile(array, repeats), axis, split_axis=dim, concat_axis=dim, tiled=True
+    )
 
 
 def contract_last(left, right):
@@ -29,7 +37,7 @@
 
 def per_device(inputs, out_grad, gate_weight, up_weight, down_weight):
     input_rows, grad_rows = (
-        lax.all_gather(inputs, "row", axis=0, tiled=True),
+        gather_from_all(inputs, "row", 0),
         lax.all_gather(out_grad, "row", axis=0, tiled=True),
     )
     gate_part = jnp.dot(input_rows, gate_weight, preferred_element_type=jnp.float32)

time: 480 us -> 455 us (0.948)
  blocking collectives: 105 us -> 62.2 us
  starting transfers between devices: 0.08 us -> 13.2 us
    all_gather x1 -> x0, blocking collectives: 56.1 us -> none  [per_device(): lax.all_gather(inputs, 'row', axis=0, tiled=True)]
    all_gather x1, blocking collectives: 48.7 us -> 62.2 us  [per_device(): lax.all_gather(out_grad, 'row', axis=0, tiled=True)]
    all_to_all x0 -> x1, starting transfers between devices: none -> 13.2 us  [gather_from_all(): lax.all_to_all(jnp.tile(array, repeats), axis, split_axis=dim, concat_axi...]
  transfers between devices with their start and end apart: 2 -> 3, of which waited for: 2 -> 2; matrix products, arithmetic and copies ran while one was open for 2% -> 2% of each run, Pallas kernels for 0% -> 0%
where the time goes in v2:
time: 455 us
  waiting for transfers between devices  343 us (75%)
  blocking collectives  62.2 us (14%)
  between operations  14.1 us (3%)
  matrix products  13.3 us (3%)
  starting transfers between devices  13.2 us (3%)
  other arithmetic  4.65 us (1%)
    reduce_scatter x1, waiting for transfers between devices, per_device(): lax.psum_scatter(contract_last(gate_grad, gate_weight) + contract_last(up...  217 us
    psum x1, waiting for transfers between devices, per_device(): lax.psum((gate_part, up_part, back_part), ('inw', 'outw'))  126 us
    all_gather x1, blocking collectives, per_device(): lax.all_gather(out_grad, 'row', axis=0, tiled=True)  62.2 us
    all_to_all x1, starting transfers between devices, gather_from_all(): lax.all_to_all(jnp.tile(array, repeats), axis, split_axis=dim, concat_axi...  13.2 us
  transfers between devices with their start and end apart: 3, of which 2 were waited for; matrix products, arithmetic and copies ran while one was open for 2% of the time, Pallas kernels for 0%

profile of v2, /device:TPU:8, one launch (start us, length us, event | category | flops | bytes accessed | tf_op | source)
XLA Modules:
  0.0 454.8 jit_solution(8008415760228083637)
XLA Ops:
  7.2 0.0 copy-start
  7.2 0.0 copy-start.4
  7.2 0.0 copy-start.3
  7.2 1.7 tile.2
  8.9 13.2 %all-to-all-start = ((bf16[32,24,512]{2,1,0:T(8,128)(2,1)}), bf16[32,24,512]{2,1,0:T(8,128)(2,1)S(1)}, u32[]{:S(2)}, u32[]{:S(2)}) async-start(bf16[32,24,512]{2,1,0:T(8,128)(2,1)} %tile.2), calls=%async_computation | async-start | bytes 1572864 | tf_op jit(solution)/shard_map/all_to_all | solution.py:10
  22.1 0.0 all-reduce.3.cloned.1.call-start
  22.2 0.0 copy-done.4
  22.2 62.2 %all_gather.3 = bf16[768,512]{1,0:T(8,128)(2,1)S(1)} all-gather(bf16[24,512]{1,0:T(8,128)(2,1)S(1)} %copy-done.4), channel_id=1, replica_groups=mesh['row'=32,'inw'=8,'outw'=2] {'row'}, dimensions={0}, use_global_device_ids=true | all-gather | bytes 811008 | tf_op jit(solution)/shard_map/all_gather | solution.py:41
  84.3 0.0 copy-done.3
  84.3 1.8 fusion.5
  86.1 0.0 copy-start.2
  86.1 0.0 all-to-all-done
  86.1 0.0 copy-done
  86.1 1.7 fusion.7
  87.8 0.0 copy-done.2
  87.8 1.8 fusion.6
  89.7 0.0 all-reduce.3.cloned.1.call-update
  89.7 0.0 reduce-scatter.2.cloned.1.call-start
  89.7 125.9 %all-reduce.3.cloned.1.call-done = (f32[768,512]{1,0:T(8,128)}, f32[768,512]{1,0:T(8,128)}, f32[768,512]{1,0:T(8,128)}) async-done(((f32[768,512]{1,0:T(8,128)}, f32[768,512]{1,0:T(8,128)}, f32[768,512]{1,0:T(8,128)}), (f32[768,512]{1,0:T(8,128)}, f32[768,512]{1,0:T(8,128)}, f32[768,512]{1,0:T(8,128)})) %all-reduce.3.cloned.1.call-update) | async-done | bytes 4718608 | tf_op jit(solution)/shard_map/psum | solution.py:46
  215.6 3.2 multiply_convert_fusion.1
  218.9 0.0 copy-start.1
  218.9 0.6 fusion.8
  219.5 0.3 copy-done.1
  219.8 1.8 convolution_add_fusion
  221.6 0.0 reduce-scatter.2.cloned.1.call-update
  221.6 0.6 fusion.1
  222.2 1.0 copy.9
  223.2 1.7 fusion.2
  224.9 1.0 copy.10
  225.9 3.3 convolution_convert_fusion
  229.2 217.4 %reduce-scatter.2.cloned.1.call-done = f32[24,512]{1,0:T(8,128)} async-done(((f32[768,512]{1,0:T(8,128)}), f32[24,512]{1,0:T(8,128)}) %reduce-scatter.2.cloned.1.call-update) | async-done | bytes 49168 | tf_op jit(solution)/shard_map/reduce_scatter | solution.py:51
  446.6 1.4 convert_element_type.29
Async XLA Ops:
  7.2 79.0 %copy-start = (bf16[512,512]{1,0:T(8,128)(2,1)S(1)}, bf16[512,512]{1,0:T(8,128)(2,1)}, u32[]{:S(2)}) copy-start(bf16[512,512]{1,0:T(8,128)(2,1)} %param.7) | copy-start | bytes 1572868
  7.2 15.0 %copy-start.4 = (bf16[24,512]{1,0:T(8,128)(2,1)S(1)}, bf16[24,512]{1,0:T(8,128)(2,1)}, u32[]{:S(2)}) copy-start(bf16[24,512]{1,0:T(8,128)(2,1)} %param.6) | copy-start | bytes 73732
  7.2 77.2 %copy-start.3 = (bf16[512,512]{1,0:T(8,128)(2,1)S(1)}, bf16[512,512]{1,0:T(8,128)(2,1)}, u32[]{:S(2)}) copy-start(bf16[512,512]{1,0:T(8,128)(2,1)} %param.9) | copy-start | bytes 1572868
  8.9 77.2 %all-to-all-start = ((bf16[32,24,512]{2,1,0:T(8,128)(2,1)}), bf16[32,24,512]{2,1,0:T(8,128)(2,1)S(1)}, u32[]{:S(2)}, u32[]{:S(2)}) async-start(bf16[32,24,512]{2,1,0:T(8,128)(2,1)} %tile.2), calls=%async_computation | async-start | bytes 1572864 | tf_op jit(solution)/shard_map/all_to_all | solution.py:10
  22.1 193.5 %all-reduce.3.cloned.1.call-start = ((), (), s32[]{:S(2)}) async-start(), calls=%async_computation.3 | async-start | bytes 9437184 | tf_op jit(solution)/shard_map/psum | solution.py:46
  86.1 1.7 copy-start.2
  89.7 356.9 %reduce-scatter.2.cloned.1.call-start = ((), (), s32[]{:S(2)}) async-start(), calls=%async_computation.2 | async-start | bytes 1622016 | tf_op jit(solution)/shard_map/reduce_scatter | solution.py:51
  218.9 0.9 copy-start.1
Sparse Core Ops, SparseCore 0:
  89.8 125.7 all-reduce.2
  221.7 224.8 reduce-scatter.1
